TPU v7x, 512 devices: a whole 4x4x16 slice. The times are simulated.
512 devices in a mesh: leaf: 16 (over z), panel: 32 (over y, x, core).
Axes of the slice: x: 4, y: 4, z: 16, core: 2. Of those that a mesh axis runs over, the one named last changes fastest.
Arguments:
- probe_low: bfloat16 [16, 4096, 256], P('leaf', 'panel'), may hold values from -6 to 6
- probe_mid: bfloat16 [16, 2048, 256], P('leaf', 'panel'), may hold values from -6 to 6
- probe_top: bfloat16 [16, 1024, 256], P('leaf', 'panel'), may hold values from -6 to 6
- inv_low: bfloat16 [16, 4096, 4096], P('leaf', 'panel'), may hold values from -0.09375 to 0.09375
- inv_mid: bfloat16 [16, 2048, 4096], P('leaf', 'panel'), may hold values from -0.09375 to 0.09375
- inv_top: bfloat16 [16, 1024, 4096], P('leaf', 'panel'), may hold values from -0.09375 to 0.09375
- gram_low: bfloat16 [16, 4096, 4096], P('leaf', 'panel'), may hold values from -0.09375 to 0.09375
- gram_mid: bfloat16 [16, 2048, 4096], P('leaf', 'panel'), may hold values from -0.09375 to 0.09375
- gram_top: bfloat16 [16, 1024, 4096], P('leaf', 'panel'), may hold values from -0.09375 to 0.09375
- panel_low: bfloat16 [16, 1024, 4096], P('leaf', 'panel'), may hold values from -0.09375 to 0.09375
- panel_mid: bfloat16 [16, 512, 4096], P('leaf', 'panel'), may hold values from -0.09375 to 0.09375
- back_low: bfloat16 [16, 4096, 1024], P('leaf', 'panel'), may hold values from -0.1875 to 0.1875
- back_mid: bfloat16 [16, 2048, 1024], P('leaf', 'panel'), may hold values from -0.1875 to 0.1875
- sep_low: int32 [16, 1024], replicated, may hold values from 0 to 4095, as said below
- sep_mid: int32 [8, 1024], replicated, may hold values from 0 to 4095, as said below
Outputs:
- half_low: bfloat16 [16, 4096, 256], P('leaf', 'panel')
- half_mid: bfloat16 [16, 2048, 256], P('leaf', 'panel')
- half_top: bfloat16 [16, 1024, 256], P('leaf', 'panel')
- solved_low: bfloat16 [16, 4096, 256], P('leaf', 'panel')
- solved_mid: bfloat16 [16, 2048, 256], P('leaf', 'panel')
- solved_top: bfloat16 [16, 1024, 256], P('leaf', 'panel')
Inputs may be any that keep to these rules, and one draw needn't show every extreme that they name: Each row of sep_low lists 1024 distinct rows of a parent supernode; 0 and 4095 occur in every row. Each row of sep_mid lists 1024 distinct rows of a parent supernode; 0 and 4095 occur in every row.
All inputs are finite; a program needn't handle non-finite values.
Results may differ from a plain program's by a relative error of at most 0.0085.
Values may be sent and summed in bfloat16 or wider, within the bound.
A program may use at most 64 MiB of HBM per device.

v0:
```python
import jax
import jax.numpy as jnp
from jax import lax
from jax.sharding import PartitionSpec as P


def from_partner(value, axis, bit):
    mask = 2**bit
    pairs = [(source, source ^ mask) for source in range(lax.axis_size(axis))]
    return lax.ppermute(value, axis, pairs)


def pair_up(block, bit):
    partner = from_partner(block, "leaf", bit)
    upper = lax.axis_index("leaf") >> bit & 1 == 1
    return jnp.where(
        upper, jnp.concatenate([partner, block], 0), jnp.concatenate([block, partner], 0)
    )


def sibling(block, bit):
    return from_partner(block, "leaf", bit)


def collect(piece, depth):
    whole = lax.all_gather(piece, "panel", axis=1, tiled=True)
    for bit in range(depth):
        whole = pair_up(whole, bit)
    return whole.reshape(-1, whole.shape[-1])


def product(matrix, rhs):
    return jnp.dot(matrix[0], rhs, preferred_element_type=jnp.float32)


def own_rows(full, depth, count):
    block = lax.axis_index("leaf") & (1 << depth) - 1
    start = (block * lax.axis_size("panel") + lax.axis_index("panel")) * count
    return lax.dynamic_slice_in_dim(full, start, count, 0)


def child_total(updates, other, rows_table, depth, height):
    child = lax.axis_index("leaf") >> depth
    own_map = lax.dynamic_index_in_dim(rows_table, child, 0, keepdims=False)
    other_map = lax.dynamic_index_in_dim(rows_table, child ^ 1, 0, keepdims=False)
    total = jnp.zeros((height, updates.shape[1]), jnp.float32)
    total = total.at[own_map].add(updates.astype(jnp.float32))
    return total.at[other_map].add(other.astype(jnp.float32))


def parent_side(updates, other, rows_table, depth, probe_local):
    count = probe_local.shape[1]
    total = child_total(
        updates, other, rows_table, depth, count * lax.axis_size("panel") * (2 << depth)
    )
    local = probe_local[0].astype(jnp.float32) - own_rows(total, depth + 1, count)
    return local.astype(jnp.bfloat16)[None]


def sweeps(
    probe_low,
    probe_mid,
    probe_top,
    inv_low,
    inv_mid,
    inv_top,
    gram_low,
    gram_mid,
    gram_top,
    panel_low,
    panel_mid,
    back_low,
    back_mid,
    sep_low,
    sep_mid,
):
    leaf_index = lax.axis_index("leaf")
    right_low = collect(probe_low, 0)
    update_low = product(panel_low, right_low).astype(jnp.bfloat16)
    update_low = collect(update_low[None], 0)
    right_mid = collect(parent_side(update_low, sibling(update_low, 0), sep_low, 0, probe_mid), 1)
    update_mid = product(panel_mid, right_mid).astype(jnp.bfloat16)
    update_mid = collect(update_mid[None], 1)
    right_top = collect(parent_side(update_mid, sibling(update_mid, 1), sep_mid, 1, probe_top), 2)
    half_low = product(inv_low, right_low).astype(jnp.bfloat16)
    half_mid = product(inv_mid, right_mid).astype(jnp.bfloat16)
    half_top = product(inv_top, right_top).astype(jnp.bfloat16)
    solved_top = product(gram_top, right_top).astype(jnp.bfloat16)
    parent_top = collect(solved_top[None], 2)
    map_mid = lax.dynamic_index_in_dim(sep_mid, leaf_index >> 1, 0, keepdims=False)
    taken_mid = jnp.take(parent_top, map_mid, axis=0)
    solved_mid = (product(gram_mid, right_mid) - product(back_mid, taken_mid)).astype(jnp.bfloat16)
    parent_mid = collect(solved_mid[None], 1)
    map_low = lax.dynamic_index_in_dim(sep_low, leaf_index, 0, keepdims=False)
    taken_low = jnp.take(parent_mid, map_low, axis=0)
    solved_low = (product(gram_low, right_low) - product(back_low, taken_low)).astype(jnp.bfloat16)
    return (
        half_low[None],
        half_mid[None],
        half_top[None],
        solved_low[None],
        solved_mid[None],
        solved_top[None],
    )


def body(
    probe_low,
    probe_mid,
    probe_top,
    inv_low,
    inv_mid,
    inv_top,
    gram_low,
    gram_mid,
    gram_top,
    panel_low,
    panel_mid,
    back_low,
    back_mid,
    sep_low,
    sep_mid,
):
    blocks_rest = (
        inv_low,
        inv_mid,
        inv_top,
        gram_low,
        gram_mid,
        gram_top,
        panel_low,
        panel_mid,
        back_low,
        back_mid,
        sep_low,
        sep_mid,
    )
    return sweeps(probe_low, probe_mid, probe_top, *blocks_rest)


def solution(mesh):
    return jax.shard_map(
        body,
        mesh=mesh,
        in_specs=(
            P("leaf", "panel", None),
            P("leaf", "panel", None),
            P("leaf", "panel", None),
            P("leaf", "panel", None),
            P("leaf", "panel", None),
            P("leaf", "panel", None),
            P("leaf", "panel", None),
            P("leaf", "panel", None),
            P("leaf", "panel", None),
            P("leaf", "panel", None),
            P("leaf", "panel", None),
            P("leaf", "panel", None),
            P("leaf", "panel", None),
            P(),
            P(),
        ),
        out_specs=(
            P("leaf", "panel", None),
            P("leaf", "panel", None),
            P("leaf", "panel", None),
            P("leaf", "panel", None),
            P("leaf", "panel", None),
            P("leaf", "panel", None),
        ),
        check_vma=False,
    )
```

profile of v0, /device:TPU:1, one launch (start us, length us, event | category | flops | bytes accessed | tf_op | source)
XLA Modules:
  0.0 584.4 jit_solution(5055272088833783193)
XLA Ops:
  7.2 0.0 copy-start
  7.2 0.0 all-gather.10.cloned.1.call-start
  7.2 0.7 all-gather.10.cloned.1.call-update
  7.9 0.0 all-gather.12.cloned.1.call-start
  8.0 68.1 %all-gather.10.cloned.1.call-done = bf16[1,4096,256]{2,1,0:T(8,128)(2,1)} async-done(((bf16[1,128,256]{2,1,0:T(8,128)(2,1)}), bf16[1,4096,256]{2,1,0:T(8,128)(2,1)}) %all-gather.10.cloned.1.call-update) | async-done | bytes 2097168 | tf_op jit(solution)/shard_map/all_gather | solution.py:26
  76.1 2.1 fusion.21
  78.2 24.0 %all-gather = bf16[1024,256]{1,0:T(8,128)(2,1)S(1)} all-gather(bf16[32,256]{1,0:T(8,128)(2,1)S(1)} %fusion.21), channel_id=2, replica_groups=mesh['leaf'=16,'panel'=32] {'panel'}, dimensions={0}, use_global_device_ids=true | all-gather | bytes 540672 | tf_op jit(solution)/shard_map/all_gather | solution.py:26
  102.2 3.2 collective-permute-start
  105.4 0.9 compare_select_fusion.2
  106.3 8.3 %scatter_custom_fusion = f32[4096,256]{1,0:T(8,128)} fusion(s32[1024]{0:T(1024)S(1)} %bitcast.132, f32[]{:T(128)} %constant.45.clone.1, bf16[1024,256]{1,0:T(8,128)(2,1)S(1)} %all-gather), kind=kCustom, calls=%fused_computation.18 | custom fusion | flops 524288 | bytes 4718596 | tf_op jit(solution)/shard_map/scatter-add | solution.py:47
  114.6 2.9 collective-permute-done
  117.5 10.2 %scatter_custom_fusion.1 = f32[4096,256]{1,0:T(8,128)} fusion(f32[4096,256]{1,0:T(8,128)} %scatter_custom_fusion, s32[1024]{0:T(1024)S(1)} %bitcast.131, bf16[1024,256]{1,0:T(8,128)(2,1)S(1)} %collective-permute-done), kind=kCustom, calls=%fused_computation.43 | custom fusion | flops 524288 | bytes 4718592 | tf_op jit(solution)/shard_map/scatter-add | solution.py:48
  127.7 1.5 fusion.49
  129.2 0.0 all-gather.12.cloned.1.call-update
  129.2 0.0 all-gather.14.cloned.1.call-start
  129.2 57.7 %all-gather.12.cloned.1.call-done = bf16[2048,256]{1,0:T(8,128)(2,1)} async-done(((bf16[64,256]{1,0:T(8,128)(2,1)}), bf16[2048,256]{1,0:T(8,128)(2,1)}) %all-gather.12.cloned.1.call-update) | async-done | bytes 1048592 | tf_op jit(solution)/shard_map/all_gather | solution.py:26
  186.9 3.2 collective-permute-start.1
  190.1 23.5 %collective-permute-done.1 = bf16[1,2048,256]{2,1,0:T(8,128)(2,1)} collective-permute-done((bf16[1,2048,256]{2,1,0:T(8,128)(2,1)}, bf16[1,2048,256]{2,1,0:T(8,128)(2,1)}, u32[]{:S(2)}, u32[]{:S(2)}) %collective-permute-start.1) | collective-permute-done | bytes 1048608 | tf_op jit(solution)/shard_map/ppermute | solution.py:10
  213.6 2.6 maximum_select_fusion
  216.2 0.4 fusion.25
  216.6 24.9 %all-gather.2 = bf16[512,256]{1,0:T(8,128)(2,1)S(1)} all-gather(bf16[16,256]{1,0:T(8,128)(2,1)S(1)} %fusion.25), channel_id=4, replica_groups=mesh['leaf'=16,'panel'=32] {'panel'}, dimensions={0}, use_global_device_ids=true | all-gather | bytes 270336 | tf_op jit(solution)/shard_map/all_gather | solution.py:26
  241.6 3.2 collective-permute-start.2
  244.8 6.5 %collective-permute-done.2 = bf16[1,512,256]{2,1,0:T(8,128)(2,1)S(1)} collective-permute-done((bf16[1,512,256]{2,1,0:T(8,128)(2,1)S(1)}, bf16[1,512,256]{2,1,0:T(8,128)(2,1)S(1)}, u32[]{:S(2)}, u32[]{:S(2)}) %collective-permute-start.2) | collective-permute-done | bytes 262176 | tf_op jit(solution)/shard_map/ppermute | solution.py:10
  251.2 0.9 maximum_select_fusion.6
  252.1 4.3 collective-permute-start.3
  256.4 0.9 compare_select_fusion.1
  257.3 8.1 %scatter_custom_fusion.2 = f32[4096,256]{1,0:T(8,128)} fusion(s32[1024]{0:T(1024)S(1)} %bitcast.134, f32[]{:T(128)} %constant.45.clone.1, bf16[1024,256]{1,0:T(8,128)(2,1)} %bitcast.20), kind=kCustom, calls=%fused_computation.16 | custom fusion | flops 524288 | bytes 4718596 | tf_op jit(solution)/shard_map/scatter-add | solution.py:47
  265.4 13.8 %collective-permute-done.3 = bf16[1024,256]{1,0:T(8,128)(2,1)} collective-permute-done((bf16[1024,256]{1,0:T(8,128)(2,1)}, bf16[1024,256]{1,0:T(8,128)(2,1)}, u32[]{:S(2)}, u32[]{:S(2)}) %collective-permute-start.3) | collective-permute-done | bytes 524320 | tf_op jit(solution)/shard_map/ppermute | solution.py:10
  279.2 10.6 %scatter_custom_fusion.3 = f32[4096,256]{1,0:T(8,128)} fusion(f32[4096,256]{1,0:T(8,128)} %scatter_custom_fusion.2, s32[1024]{0:T(1024)S(1)} %bitcast.133, bf16[1024,256]{1,0:T(8,128)(2,1)} %collective-permute-done.3), kind=kCustom, calls=%fused_computation.40 | custom fusion | flops 524288 | bytes 4718592 | tf_op jit(solution)/shard_map/scatter-add | solution.py:48
  289.8 0.8 fusion.50
  290.6 24.0 %all-gather.3 = bf16[1024,256]{1,0:T(8,128)(2,1)S(1)} all-gather(bf16[32,256]{1,0:T(8,128)(2,1)S(1)} %fusion.50), channel_id=5, replica_groups=mesh['leaf'=16,'panel'=32] {'panel'}, dimensions={0}, use_global_device_ids=true | all-gather | bytes 540672 | tf_op jit(solution)/shard_map/all_gather | solution.py:26
  314.5 2.2 collective-permute-start.4
  316.8 13.0 %collective-permute-done.4 = bf16[1,1024,256]{2,1,0:T(8,128)(2,1)S(1)} collective-permute-done((bf16[1,1024,256]{2,1,0:T(8,128)(2,1)S(1)}, bf16[1,1024,256]{2,1,0:T(8,128)(2,1)S(1)}, u32[]{:S(2)}, u32[]{:S(2)}) %collective-permute-start.4) | collective-permute-done | bytes 524320 | tf_op jit(solution)/shard_map/ppermute | solution.py:10
  329.8 1.2 maximum_select_fusion.4
  330.9 4.1 collective-permute-start.5
  335.1 45.6 %collective-permute-done.5 = bf16[2,1024,256]{2,1,0:T(8,128)(2,1)} collective-permute-done((bf16[2,1024,256]{2,1,0:T(8,128)(2,1)}, bf16[2,1024,256]{2,1,0:T(8,128)(2,1)}, u32[]{:S(2)}, u32[]{:S(2)}) %collective-permute-start.5) | collective-permute-done | bytes 1048608 | tf_op jit(solution)/shard_map/ppermute | solution.py:10
  380.7 2.6 maximum_select_fusion.1
  383.3 0.5 convolution_convert_fusion.1
  383.8 0.0 copy-start.10
  383.8 25.3 %all-gather.4 = bf16[1024,256]{1,0:T(8,128)(2,1)S(1)} all-gather(bf16[32,256]{1,0:T(8,128)(2,1)S(1)} %bitcast.125), channel_id=6, replica_groups=mesh['leaf'=16,'panel'=32] {'panel'}, dimensions={0}, use_global_device_ids=true | all-gather | bytes 540672 | tf_op jit(solution)/shard_map/all_gather | solution.py:26
  409.1 2.2 collective-permute-start.6
  411.3 13.1 %collective-permute-done.6 = bf16[1,1024,256]{2,1,0:T(8,128)(2,1)S(1)} collective-permute-done((bf16[1,1024,256]{2,1,0:T(8,128)(2,1)S(1)}, bf16[1,1024,256]{2,1,0:T(8,128)(2,1)S(1)}, u32[]{:S(2)}, u32[]{:S(2)}) %collective-permute-start.6) | collective-permute-done | bytes 524320 | tf_op jit(solution)/shard_map/ppermute | solution.py:10
  424.3 0.2 maximum_select_fusion.5
  424.5 4.1 collective-permute-start.7
  428.6 45.4 %collective-permute-done.7 = bf16[2,1024,256]{2,1,0:T(8,128)(2,1)S(1)} collective-permute-done((bf16[2,1024,256]{2,1,0:T(8,128)(2,1)S(1)}, bf16[2,1024,256]{2,1,0:T(8,128)(2,1)S(1)}, u32[]{:S(2)}, u32[]{:S(2)}) %collective-permute-start.7) | collective-permute-done | bytes 1048608 | tf_op jit(solution)/shard_map/ppermute | solution.py:10
  474.0 1.6 maximum_select_fusion.2
  475.7 6.5 %gather_fusion = bf16[1024,256]{1,0:T(8,128)(2,1)} fusion(bf16[4096,256]{1,0:T(8,128)(2,1)} %bitcast.111, s32[1024]{0:T(1024)S(1)} %fusion.51), kind=kCustom, calls=%fused_computation.clone | custom fusion | bytes 1052672 | tf_op jit(solution)/shard_map/jit(_take)/gather | solution.py:91
  482.1 1.4 fusion.37
  483.5 2.1 fusion.19
  485.7 0.0 all-gather.14.cloned.1.call-update
  485.7 0.8 constant_dynamic-slice_fusion
  486.5 57.2 %all-gather.14.cloned.1.call-done = bf16[2048,256]{1,0:T(8,128)(2,1)} async-done(((bf16[64,256]{1,0:T(8,128)(2,1)}), bf16[2048,256]{1,0:T(8,128)(2,1)}) %all-gather.14.cloned.1.call-update) | async-done | bytes 1048592 | tf_op jit(solution)/shard_map/all_gather | solution.py:26
  543.6 3.4 collective-permute-start.8
  547.1 2.7 fusion.16
  549.8 0.4 fusion
  550.2 0.6 copy-done.6
  550.8 1.1 fusion.20
  551.9 0.5 copy-done.3
  552.4 1.1 fusion.24
  553.5 17.0 %collective-permute-done.8 = bf16[1,2048,256]{2,1,0:T(8,128)(2,1)S(1)} collective-permute-done((bf16[1,2048,256]{2,1,0:T(8,128)(2,1)}, bf16[1,2048,256]{2,1,0:T(8,128)(2,1)S(1)}, u32[]{:S(2)}, u32[]{:S(2)}) %collective-permute-start.8) | collective-permute-done | bytes 1048608 | tf_op jit(solution)/shard_map/ppermute | solution.py:10
  570.5 0.3 maximum_select_fusion.3
  570.9 0.0 copy-start.13
  570.9 4.9 gather_fusion.1
  575.8 2.1 fusion.15
  (29 shorter events, 0.1 us)
Async XLA Ops:
  7.2 539.9 %copy-start = (bf16[1,128,4096]{2,1,0:T(8,128)(2,1)S(1)}, bf16[1,128,4096]{2,1,0:T(8,128)(2,1)}, u32[]{:S(2)}) copy-start(bf16[1,128,4096]{2,1,0:T(8,128)(2,1)} %param.20) | copy-start | bytes 3145732
  7.2 68.9 %all-gather.10.cloned.1.call-start = ((), (), s32[]{:S(2)}) async-start(), calls=%async_computation | async-start | bytes 2162688 | tf_op jit(solution)/shard_map/all_gather | solution.py:26
  7.9 179.0 %all-gather.12.cloned.1.call-start = ((), (), s32[]{:S(2)}) async-start(), calls=%async_computation.1 | async-start | bytes 1081344 | tf_op jit(solution)/shard_map/all_gather | solution.py:26
  102.2 15.3 %collective-permute-start = (bf16[1024,256]{1,0:T(8,128)(2,1)S(1)}, bf16[1024,256]{1,0:T(8,128)(2,1)S(1)}, u32[]{:S(2)}, u32[]{:S(2)}) collective-permute-start(bf16[1024,256]{1,0:T(8,128)(2,1)S(1)} %all-gather), channel_id=1, source_target_pairs={{0,32},{32,0},{64,96},{96,64},{128,160},{160,128},{192,224},{224,1... | collective-permute-start | bytes 1572872 | tf_op jit(solution)/shard_map/ppermute | solution.py:10
  117.5 10.2 %copy-start.11 = (bf16[1,64,256]{2,1,0:T(8,128)(2,1)S(1)}, bf16[1,64,256]{2,1,0:T(8,128)(2,1)}, u32[]{:S(2)}) copy-start(bf16[1,64,256]{2,1,0:T(8,128)(2,1)} %param.18) | copy-start | bytes 98308
  129.2 414.4 %all-gather.14.cloned.1.call-start = ((), (), s32[]{:S(2)}) async-start(), calls=%async_computation.2 | async-start | bytes 1081344 | tf_op jit(solution)/shard_map/all_gather | solution.py:26
  186.9 26.7 %collective-permute-start.1 = (bf16[1,2048,256]{2,1,0:T(8,128)(2,1)}, bf16[1,2048,256]{2,1,0:T(8,128)(2,1)}, u32[]{:S(2)}, u32[]{:S(2)}) collective-permute-start(bf16[1,2048,256]{2,1,0:T(8,128)(2,1)} %bitcast.119), channel_id=1, source_target_pairs={{0,32},{32,0},{64,96},{96,64},{128,160},{160,128},{192,224},{224,1... | collective-permute-start | bytes 3145736 | tf_op jit(solution)/shard_map/ppermute | solution.py:10
  190.1 26.2 %copy-start.9 = (bf16[1,16,4096]{2,1,0:T(8,128)(2,1)S(1)}, bf16[1,16,4096]{2,1,0:T(8,128)(2,1)}, u32[]{:S(2)}) copy-start(bf16[1,16,4096]{2,1,0:T(8,128)(2,1)} %param.27) | copy-start | bytes 393220
  241.6 9.6 %collective-permute-start.2 = (bf16[1,512,256]{2,1,0:T(8,128)(2,1)S(1)}, bf16[1,512,256]{2,1,0:T(8,128)(2,1)S(1)}, u32[]{:S(2)}, u32[]{:S(2)}) collective-permute-start(bf16[1,512,256]{2,1,0:T(8,128)(2,1)S(1)} %bitcast.121), channel_id=1, source_target_pairs={{0,32},{32,0},{64,96},{96,64},{128,160},{160,128},{192,224},{224,1... | collective-permute-start | bytes 786440 | tf_op jit(solution)/shard_map/ppermute | solution.py:10
  252.1 27.1 %collective-permute-start.3 = (bf16[1024,256]{1,0:T(8,128)(2,1)}, bf16[1024,256]{1,0:T(8,128)(2,1)}, u32[]{:S(2)}, u32[]{:S(2)}) collective-permute-start(bf16[1024,256]{1,0:T(8,128)(2,1)} %bitcast.20), channel_id=1, source_target_pairs={{0,64},{32,96},{64,0},{96,32},{128,192},{160,224},{192,128},{224,1... | collective-permute-start | bytes 1572872 | tf_op jit(solution)/shard_map/ppermute | solution.py:10
  279.2 10.6 %copy-start.12 = (bf16[1,32,256]{2,1,0:T(8,128)(2,1)S(1)}, bf16[1,32,256]{2,1,0:T(8,128)(2,1)}, u32[]{:S(2)}) copy-start(bf16[1,32,256]{2,1,0:T(8,128)(2,1)} %param.19) | copy-start | bytes 49156
  314.5 15.3 %collective-permute-start.4 = (bf16[1,1024,256]{2,1,0:T(8,128)(2,1)S(1)}, bf16[1,1024,256]{2,1,0:T(8,128)(2,1)S(1)}, u32[]{:S(2)}, u32[]{:S(2)}) collective-permute-start(bf16[1,1024,256]{2,1,0:T(8,128)(2,1)S(1)} %bitcast.113), channel_id=1, source_target_pairs={{0,32},{32,0},{64,96},{96,64},{128,160},{160,128},{192,224},{224,1... | collective-permute-start | bytes 1572872 | tf_op jit(solution)/shard_map/ppermute | solution.py:10
  330.9 49.8 %collective-permute-start.5 = (bf16[2,1024,256]{2,1,0:T(8,128)(2,1)}, bf16[2,1024,256]{2,1,0:T(8,128)(2,1)}, u32[]{:S(2)}, u32[]{:S(2)}) collective-permute-start(bf16[2,1024,256]{2,1,0:T(8,128)(2,1)} %maximum_select_fusion.4), channel_id=1, source_target_pairs={{0,64},{32,96},{64,0},{96,32},{128,192},{160,224},{192,128},{224,1... | collective-permute-start | bytes 3145736 | tf_op jit(solution)/shard_map/ppermute | solution.py:10
  335.1 48.3 %copy-start.7 = (bf16[1,32,4096]{2,1,0:T(8,128)(2,1)S(1)}, bf16[1,32,4096]{2,1,0:T(8,128)(2,1)}, u32[]{:S(2)}) copy-start(bf16[1,32,4096]{2,1,0:T(8,128)(2,1)} %param.25) | copy-start | bytes 786436
  383.3 41.2 %copy-start.2 = (bf16[4,1024,256]{2,1,0:T(8,128)(2,1)}, bf16[4,1024,256]{2,1,0:T(8,128)(2,1)S(1)}, u32[]{:S(2)}) copy-start(bf16[4,1024,256]{2,1,0:T(8,128)(2,1)S(1)} %maximum_select_fusion.1) | copy-start | bytes 6291460
  383.8 91.9 %copy-start.10 = (bf16[256,32]{0,1:T(8,128)(2,1)}, bf16[256,32]{0,1:T(8,128)(2,1)S(1)}, u32[]{:S(2)}) copy-start(bf16[256,32]{0,1:T(8,128)(2,1)S(1)} %convolution_convert_fusion.1) | copy-start | bytes 49156
  409.1 15.3 %collective-permute-start.6 = (bf16[1,1024,256]{2,1,0:T(8,128)(2,1)S(1)}, bf16[1,1024,256]{2,1,0:T(8,128)(2,1)S(1)}, u32[]{:S(2)}, u32[]{:S(2)}) collective-permute-start(bf16[1,1024,256]{2,1,0:T(8,128)(2,1)S(1)} %bitcast.115), channel_id=1, source_target_pairs={{0,32},{32,0},{64,96},{96,64},{128,160},{160,128},{192,224},{224,1... | collective-permute-start | bytes 1572872 | tf_op jit(solution)/shard_map/ppermute | solution.py:10
  424.5 49.5 %collective-permute-start.7 = (bf16[2,1024,256]{2,1,0:T(8,128)(2,1)S(1)}, bf16[2,1024,256]{2,1,0:T(8,128)(2,1)S(1)}, u32[]{:S(2)}, u32[]{:S(2)}) collective-permute-start(bf16[2,1024,256]{2,1,0:T(8,128)(2,1)S(1)} %maximum_select_fusion.5), channel_id=1, source_target_pairs={{0,64},{32,96},{64,0},{96,32},{128,192},{160,224},{192,128},{224,1... | collective-permute-start | bytes 3145736 | tf_op jit(solution)/shard_map/ppermute | solution.py:10
  475.7 6.5 %copy-start.14 = (bf16[1,64,1024]{2,1,0:T(8,128)(2,1)S(1)}, bf16[1,64,1024]{2,1,0:T(8,128)(2,1)}, u32[]{:S(2)}) copy-start(bf16[1,64,1024]{2,1,0:T(8,128)(2,1)} %param.29) | copy-start | bytes 393220
  543.6 6.1 %copy-start.1 = (bf16[1,4096,256]{2,1,0:T(8,128)(2,1)S(1)}, bf16[1,4096,256]{2,1,0:T(8,128)(2,1)}, u32[]{:S(2)}) copy-start(bf16[1,4096,256]{2,1,0:T(8,128)(2,1)} %all-gather.10.cloned.1.call-done) | copy-start | bytes 6291460
  543.6 6.1 %copy-start.4 = (bf16[1,128,4096]{2,1,0:T(8,128)(2,1)S(1)}, bf16[1,128,4096]{2,1,0:T(8,128)(2,1)}, u32[]{:S(2)}) copy-start(bf16[1,128,4096]{2,1,0:T(8,128)(2,1)} %param.23) | copy-start | bytes 3145732
  543.6 26.9 %collective-permute-start.8 = (bf16[1,2048,256]{2,1,0:T(8,128)(2,1)}, bf16[1,2048,256]{2,1,0:T(8,128)(2,1)S(1)}, u32[]{:S(2)}, u32[]{:S(2)}) collective-permute-start(bf16[1,2048,256]{2,1,0:T(8,128)(2,1)} %bitcast.117), channel_id=1, source_target_pairs={{0,32},{32,0},{64,96},{96,64},{128,160},{160,128},{192,224},{224,1... | collective-permute-start | bytes 3145736 | tf_op jit(solution)/shard_map/ppermute | solution.py:10
  549.8 1.0 copy-start.6
  549.8 2.1 copy-start.8
  550.8 1.6 copy-start.3
  550.8 19.7 %copy-start.5 = (bf16[2048,256]{1,0:T(8,128)(2,1)S(1)}, bf16[2048,256]{1,0:T(8,128)(2,1)}, u32[]{:S(2)}) copy-start(bf16[2048,256]{1,0:T(8,128)(2,1)} %all-gather.14.cloned.1.call-done) | copy-start | bytes 3145732
  570.9 5.0 copy-start.13
Sparse Core Ops, SparseCore 0:
  11.2 64.8 all-gather.9
  129.3 57.5 all-gather.11
  485.8 57.7 all-gather.13
where the time goes:
time: 585 us; the launch traced here: 584 us
  waiting for transfers between devices  364 us (62%)
  blocking collectives  98.2 us (17%)
  other arithmetic  50.5 us (9%)
  starting transfers between devices  30.1 us (5%)
  between operations  14 us (2%)
  matrix products  13.8 us (2%)
  local copies, waits for them, and re-layouts  13.4 us (2%)
    all_gather x3, waiting for transfers between devices, collect(): whole = lax.all_gather(piece, 'panel', axis=1, tiled=True)  183 us
    ppermute x9, waiting for transfers between devices, from_partner(): return lax.ppermute(value, axis, pairs)  181 us
    all_gather x4, blocking collectives, collect(): whole = lax.all_gather(piece, 'panel', axis=1, tiled=True)  98.2 us
    ppermute x9, starting transfers between devices, from_partner(): return lax.ppermute(value, axis, pairs)  29.9 us
    scatter-add x2, other arithmetic, child_total(): return total.at[other_map].add(other.astype(jnp.float32))  20.8 us
    scatter-add x2, other arithmetic, child_total(): total = total.at[own_map].add(updates.astype(jnp.float32))  16.4 us
    dot_general x10, matrix products, product(): return jnp.dot(matrix[0], rhs, preferred_element_type=jnp.float32)  13.8 us
  transfers between devices with their start and end apart: 12, of which 12 were waited for; matrix products, arithmetic and copies ran while one was open for 4% of the time, Pallas kernels for 0%

commit v1 on v0

--- a/solution.py
+++ b/solution.py
@@ -2,6 +2,13 @@
 import jax.numpy as jnp
 from jax import lax
 from jax.sharding import PartitionSpec as P
+
+
+def all_by_exchange(x, name, along):
+    devices = lax.axis_size(name)
+    blocks = jnp.stack([x for _ in range(devices)])
+    blocks = lax.all_to_all(blocks, name, split_axis=0, concat_axis=0)
+    return jnp.concatenate(blocks, axis=along)
 
 
 def from_partner(value, axis, bit):
@@ -23,7 +30,7 @@
 
 
 def collect(piece, depth):
-    whole = lax.all_gather(piece, "panel", axis=1, tiled=True)
+    whole = all_by_exchange(piece, "panel", 1)
     for bit in range(depth):
         whole = pair_up(whole, bit)
     return whole.reshape(-1, whole.shape[-1])

time: 585 us -> 438 us (0.75)
  waiting for transfers between devices: 364 us -> 205 us
  blocking collectives: 98.2 us -> 122 us
  between operations: 14 us -> 0.96 us
    all_gather x3 -> x0, waiting for transfers between devices: 183 us -> none  [collect(): whole = lax.all_gather(piece, 'panel', axis=1, tiled=True)]
    all_to_all x0 -> x6, blocking collectives: none -> 122 us  [all_by_exchange(): blocks = lax.all_to_all(blocks, name, split_axis=0, concat_axis=0)]
    all_gather x4 -> x0, blocking collectives: 98.2 us -> none  [collect(): whole = lax.all_gather(piece, 'panel', axis=1, tiled=True)]
    all_to_all x0 -> x1, waiting for transfers between devices: none -> 16.6 us  [all_by_exchange(): blocks = lax.all_to_all(blocks, name, split_axis=0, concat_axis=0)]
    ppermute x9, waiting for transfers between devices: 181 us -> 189 us  [from_partner(): return lax.ppermute(value, axis, pairs)]
    ppermute x9, starting transfers between devices: 29.9 us -> 23.4 us  [from_partner(): return lax.ppermute(value, axis, pairs)]
  transfers between devices with their start and end apart: 12 -> 10, of which waited for: 12 -> 10; matrix products, arithmetic and copies ran while one was open for 4% -> 5% of each run, Pallas kernels for 0% -> 0%
where the time goes in v1:
time: 438 us; the launch traced here: 436 us
  waiting for transfers between devices  205 us (47%)
  blocking collectives  122 us (28%)
  other arithmetic  51.7 us (12%)
  starting transfers between devices  28.2 us (6%)
  local copies, waits for them, and re-layouts  17.9 us (4%)
  matrix products  10.7 us (2%)
    ppermute x9, waiting for transfers between devices, from_partner(): return lax.ppermute(value, axis, pairs)  189 us
    all_to_all x6, blocking collectives, all_by_exchange(): blocks = lax.all_to_all(blocks, name, split_axis=0, concat_axis=0)  122 us
    ppermute x9, starting transfers between devices, from_partner(): return lax.ppermute(value, axis, pairs)  23.4 us
    scatter-add x2, other arithmetic, child_total(): return total.at[other_map].add(other.astype(jnp.float32))  21.2 us
    all_to_all x1, waiting for transfers between devices, all_by_exchange(): blocks = lax.all_to_all(blocks, name, split_axis=0, concat_axis=0)  16.6 us
    scatter-add x2, other arithmetic, child_total(): total = total.at[own_map].add(updates.astype(jnp.float32))  16.3 us
    select_n x7, other arithmetic, pair_up(): jnp.where(upper, jnp.concatenate([partner, block], 0), jnp.concatenate([b...  10.8 us
    dot_general x10, matrix products, product(): return jnp.dot(matrix[0], rhs, preferred_element_type=jnp.float32)  10.7 us
  transfers between devices with their start and end apart: 10, of which 10 were waited for; matrix products, arithmetic and copies ran while one was open for 5% of the time, Pallas kernels for 0%

profile of v1, /device:TPU:1, one launch (start us, length us, event | category | flops | bytes accessed | tf_op | source)
XLA Modules:
  0.0 436.4 jit_solution(11515218564930025843)
XLA Ops:
  0.6 1.2 stack.14
  1.8 38.2 %all_to_all.35 = bf16[32,1,128,256]{3,2,1,0:T(8,128)(2,1)S(1)} all-to-all(bf16[32,1,128,256]{3,2,1,0:T(8,128)(2,1)S(1)} %stack.14), channel_id=1, replica_groups=mesh['leaf'=16,'panel'=32] {'panel'}, dimensions={0} | all-to-all | bytes 4194304 | tf_op jit(solution)/shard_map/all_to_all | solution.py:10
  40.0 0.5 convolution_convert_fusion.4
  40.5 0.1 stack.15
  40.6 15.4 %all_to_all.36 = bf16[32,1,32,256]{3,2,1,0:T(8,128)(2,1)} all-to-all(bf16[32,1,32,256]{3,2,1,0:T(8,128)(2,1)S(1)} %stack.15), channel_id=1, replica_groups=mesh['leaf'=16,'panel'=32] {'panel'}, dimensions={0} | all-to-all | bytes 1048576 | tf_op jit(solution)/shard_map/all_to_all | solution.py:10
  55.9 2.3 collective-permute-start
  58.2 0.9 compare_select_fusion.2
  59.1 8.2 %scatter_custom_fusion = f32[4096,256]{1,0:T(8,128)} fusion(s32[1024]{0:T(1024)S(1)} %bitcast.125, f32[]{:T(128)} %constant.45.clone.1, bf16[1024,256]{1,0:T(8,128)(2,1)} %bitcast.8), kind=kCustom, calls=%fused_computation.12 | custom fusion | flops 524288 | bytes 4718596 | tf_op jit(solution)/shard_map/scatter-add | solution.py:54
  67.2 4.0 collective-permute-done
  71.2 10.6 %scatter_custom_fusion.1 = f32[4096,256]{1,0:T(8,128)} fusion(f32[4096,256]{1,0:T(8,128)} %scatter_custom_fusion, s32[1024]{0:T(1024)S(1)} %bitcast.124, bf16[1024,256]{1,0:T(8,128)(2,1)} %collective-permute-done), kind=kCustom, calls=%fused_computation.38 | custom fusion | flops 524288 | bytes 4718592 | tf_op jit(solution)/shard_map/scatter-add | solution.py:55
  81.8 0.8 fusion.36
  82.7 0.1 stack.16
  82.8 21.9 %all_to_all.37 = bf16[32,1,64,256]{3,2,1,0:T(8,128)(2,1)} all-to-all(bf16[32,1,64,256]{3,2,1,0:T(8,128)(2,1)S(1)} %stack.16), channel_id=1, replica_groups=mesh['leaf'=16,'panel'=32] {'panel'}, dimensions={0} | all-to-all | bytes 2097152 | tf_op jit(solution)/shard_map/all_to_all | solution.py:10
  104.7 2.3 collective-permute-start.1
  107.0 24.3 %collective-permute-done.1 = bf16[1,2048,256]{2,1,0:T(8,128)(2,1)} collective-permute-done((bf16[1,2048,256]{2,1,0:T(8,128)(2,1)}, bf16[1,2048,256]{2,1,0:T(8,128)(2,1)}, u32[]{:S(2)}, u32[]{:S(2)}) %collective-permute-start.1) | collective-permute-done | bytes 1048608 | tf_op jit(solution)/shard_map/ppermute | solution.py:17
  131.2 2.6 maximum_select_fusion
  133.8 1.3 copy-done.1
  135.2 0.4 fusion.11
  135.6 13.2 %all_to_all.38 = bf16[32,1,16,256]{3,2,1,0:T(8,128)(2,1)S(1)} all-to-all(bf16[32,1,16,256]{3,2,1,0:T(8,128)(2,1)S(1)} %stack.17), channel_id=1, replica_groups=mesh['leaf'=16,'panel'=32] {'panel'}, dimensions={0} | all-to-all | bytes 524288 | tf_op jit(solution)/shard_map/all_to_all | solution.py:10
  148.8 2.3 collective-permute-start.2
  151.1 7.3 %collective-permute-done.2 = bf16[1,512,256]{2,1,0:T(8,128)(2,1)S(1)} collective-permute-done((bf16[1,512,256]{2,1,0:T(8,128)(2,1)S(1)}, bf16[1,512,256]{2,1,0:T(8,128)(2,1)S(1)}, u32[]{:S(2)}, u32[]{:S(2)}) %collective-permute-start.2) | collective-permute-done | bytes 262176 | tf_op jit(solution)/shard_map/ppermute | solution.py:17
  158.4 0.9 maximum_select_fusion.6
  159.2 3.8 collective-permute-start.3
  163.1 0.9 compare_select_fusion.1
  163.9 8.2 %scatter_custom_fusion.2 = f32[4096,256]{1,0:T(8,128)} fusion(s32[1024]{0:T(1024)S(1)} %bitcast.127, f32[]{:T(128)} %constant.45.clone.1, bf16[1024,256]{1,0:T(8,128)(2,1)} %bitcast.22), kind=kCustom, calls=%fused_computation.10 | custom fusion | flops 524288 | bytes 4718596 | tf_op jit(solution)/shard_map/scatter-add | solution.py:54
  172.1 14.6 %collective-permute-done.3 = bf16[1024,256]{1,0:T(8,128)(2,1)} collective-permute-done((bf16[1024,256]{1,0:T(8,128)(2,1)}, bf16[1024,256]{1,0:T(8,128)(2,1)}, u32[]{:S(2)}, u32[]{:S(2)}) %collective-permute-start.3) | collective-permute-done | bytes 524320 | tf_op jit(solution)/shard_map/ppermute | solution.py:17
  186.6 10.6 %scatter_custom_fusion.3 = f32[4096,256]{1,0:T(8,128)} fusion(f32[4096,256]{1,0:T(8,128)} %scatter_custom_fusion.2, s32[1024]{0:T(1024)S(1)} %bitcast.126, bf16[1024,256]{1,0:T(8,128)(2,1)} %collective-permute-done.3), kind=kCustom, calls=%fused_computation.35 | custom fusion | flops 524288 | bytes 4718592 | tf_op jit(solution)/shard_map/scatter-add | solution.py:55
  197.3 0.8 fusion.37
  198.0 0.1 stack.18
  198.1 16.4 %all_to_all.39 = bf16[32,1,32,256]{3,2,1,0:T(8,128)(2,1)S(1)} all-to-all(bf16[32,1,32,256]{3,2,1,0:T(8,128)(2,1)S(1)} %stack.18), channel_id=1, replica_groups=mesh['leaf'=16,'panel'=32] {'panel'}, dimensions={0} | all-to-all | bytes 1048576 | tf_op jit(solution)/shard_map/all_to_all | solution.py:10
  214.5 1.9 collective-permute-start.4
  216.4 13.0 %collective-permute-done.4 = bf16[1,1024,256]{2,1,0:T(8,128)(2,1)S(1)} collective-permute-done((bf16[1,1024,256]{2,1,0:T(8,128)(2,1)S(1)}, bf16[1,1024,256]{2,1,0:T(8,128)(2,1)S(1)}, u32[]{:S(2)}, u32[]{:S(2)}) %collective-permute-start.4) | collective-permute-done | bytes 524320 | tf_op jit(solution)/shard_map/ppermute | solution.py:17
  229.4 1.1 maximum_select_fusion.4
  230.6 3.8 collective-permute-start.5
  234.4 46.3 %collective-permute-done.5 = bf16[2,1024,256]{2,1,0:T(8,128)(2,1)} collective-permute-done((bf16[2,1024,256]{2,1,0:T(8,128)(2,1)}, bf16[2,1024,256]{2,1,0:T(8,128)(2,1)}, u32[]{:S(2)}, u32[]{:S(2)}) %collective-permute-start.5) | collective-permute-done | bytes 1048608 | tf_op jit(solution)/shard_map/ppermute | solution.py:17
  280.7 2.6 maximum_select_fusion.1
  283.3 0.5 convolution_convert_fusion.2
  283.7 0.1 stack.19
  283.8 16.6 %all_to_all.40 = bf16[32,1,32,256]{3,2,1,0:T(8,128)(2,1)S(1)} all-to-all(bf16[32,1,32,256]{3,2,1,0:T(8,128)(2,1)S(1)} %stack.19), channel_id=1, replica_groups=mesh['leaf'=16,'panel'=32] {'panel'}, dimensions={0} | all-to-all | bytes 1048576 | tf_op jit(solution)/shard_map/all_to_all | solution.py:10
  300.4 1.9 collective-permute-start.6
  302.4 13.0 %collective-permute-done.6 = bf16[1,1024,256]{2,1,0:T(8,128)(2,1)S(1)} collective-permute-done((bf16[1,1024,256]{2,1,0:T(8,128)(2,1)S(1)}, bf16[1,1024,256]{2,1,0:T(8,128)(2,1)S(1)}, u32[]{:S(2)}, u32[]{:S(2)}) %collective-permute-start.6) | collective-permute-done | bytes 524320 | tf_op jit(solution)/shard_map/ppermute | solution.py:17
  315.4 0.2 maximum_select_fusion.5
  315.6 3.1 collective-permute-start.7
  318.7 47.1 %collective-permute-done.7 = bf16[2,1024,256]{2,1,0:T(8,128)(2,1)S(1)} collective-permute-done((bf16[2,1024,256]{2,1,0:T(8,128)(2,1)S(1)}, bf16[2,1024,256]{2,1,0:T(8,128)(2,1)S(1)}, u32[]{:S(2)}, u32[]{:S(2)}) %collective-permute-start.7) | collective-permute-done | bytes 1048608 | tf_op jit(solution)/shard_map/ppermute | solution.py:17
  365.9 1.6 maximum_select_fusion.2
  367.5 6.5 %gather_fusion = bf16[1024,256]{1,0:T(8,128)(2,1)} fusion(bf16[4096,256]{1,0:T(8,128)(2,1)} %bitcast.107, s32[1024]{0:T(1024)S(1)} %fusion.38), kind=kCustom, calls=%fused_computation.clone | custom fusion | bytes 1052672 | tf_op jit(solution)/shard_map/jit(_take)/gather | solution.py:98
  374.0 1.4 fusion.24
  375.4 2.2 fusion.8
  377.6 1.1 stack.20
  378.8 4.8 %all-to-all-start.6 = ((bf16[32,1,64,256]{3,2,1,0:T(8,128)(2,1)}), bf16[32,1,64,256]{3,2,1,0:T(8,128)(2,1)}, u32[]{:S(2)}, u32[]{:S(2)}) async-start(bf16[32,1,64,256]{3,2,1,0:T(8,128)(2,1)} %stack.20), calls=%async_computation.6 | async-start | bytes 2097152 | tf_op jit(solution)/shard_map/all_to_all | solution.py:10
  383.6 0.8 constant_dynamic-slice_fusion
  384.4 16.6 %all-to-all-done.6 = bf16[32,1,64,256]{3,2,1,0:T(8,128)(2,1)} async-done(((bf16[32,1,64,256]{3,2,1,0:T(8,128)(2,1)}), bf16[32,1,64,256]{3,2,1,0:T(8,128)(2,1)}, u32[]{:S(2)}, u32[]{:S(2)}) %all-to-all-start.6) | async-done | bytes 1048608 | tf_op jit(solution)/shard_map/all_to_all | solution.py:10
  400.9 2.0 collective-permute-start.8
  403.0 1.1 fusion.7
  404.1 0.4 fusion.12
  404.5 1.1 copy-done.2
  405.7 0.1 copy-done.6
  405.7 1.1 fusion.9
  406.8 0.5 copy-done.4
  407.4 1.1 fusion.10
  408.4 19.1 %collective-permute-done.8 = bf16[1,2048,256]{2,1,0:T(8,128)(2,1)S(1)} collective-permute-done((bf16[1,2048,256]{2,1,0:T(8,128)(2,1)}, bf16[1,2048,256]{2,1,0:T(8,128)(2,1)S(1)}, u32[]{:S(2)}, u32[]{:S(2)}) %collective-permute-start.8) | collective-permute-done | bytes 1048608 | tf_op jit(solution)/shard_map/ppermute | solution.py:17
  427.5 1.9 maximum_select_fusion.3
  429.3 4.9 %gather_fusion.1 = bf16[1024,256]{1,0:T(8,128)(2,1)} fusion(bf16[4096,256]{1,0:T(8,128)(2,1)S(1)} %bitcast.108, s32[1024]{0:T(1024)S(1)} %fusion.39), kind=kCustom, calls=%fused_computation.1.clone | custom fusion | bytes 1052672 | tf_op jit(solution)/shard_map/jit(_take)/gather | solution.py:102
  434.3 2.1 fusion.6
  (33 shorter events, 0.1 us)
Async XLA Ops:
  0.6 402.3 %copy-start = (bf16[1,128,4096]{2,1,0:T(8,128)(2,1)S(1)}, bf16[1,128,4096]{2,1,0:T(8,128)(2,1)}, u32[]{:S(2)}) copy-start(bf16[1,128,4096]{2,1,0:T(8,128)(2,1)} %param.20) | copy-start | bytes 3145732
  1.8 38.2 %copy-start.7 = (bf16[1,32,4096]{2,1,0:T(8,128)(2,1)S(1)}, bf16[1,32,4096]{2,1,0:T(8,128)(2,1)}, u32[]{:S(2)}) copy-start(bf16[1,32,4096]{2,1,0:T(8,128)(2,1)} %param.26) | copy-start | bytes 786436
  55.9 15.2 %collective-permute-start = (bf16[1024,256]{1,0:T(8,128)(2,1)}, bf16[1024,256]{1,0:T(8,128)(2,1)}, u32[]{:S(2)}, u32[]{:S(2)}) collective-permute-start(bf16[1024,256]{1,0:T(8,128)(2,1)} %bitcast.8), channel_id=1, source_target_pairs={{0,32},{32,0},{64,96},{96,64},{128,160},{160,128},{192,224},{224,1... | collective-permute-start | bytes 1572872 | tf_op jit(solution)/shard_map/ppermute | solution.py:17
  71.2 10.6 %copy-start.13 = (bf16[1,64,256]{2,1,0:T(8,128)(2,1)S(1)}, bf16[1,64,256]{2,1,0:T(8,128)(2,1)}, u32[]{:S(2)}) copy-start(bf16[1,64,256]{2,1,0:T(8,128)(2,1)} %param.18) | copy-start | bytes 98308
  104.7 26.5 %collective-permute-start.1 = (bf16[1,2048,256]{2,1,0:T(8,128)(2,1)}, bf16[1,2048,256]{2,1,0:T(8,128)(2,1)}, u32[]{:S(2)}, u32[]{:S(2)}) collective-permute-start(bf16[1,2048,256]{2,1,0:T(8,128)(2,1)} %bitcast.11), channel_id=1, source_target_pairs={{0,32},{32,0},{64,96},{96,64},{128,160},{160,128},{192,224},{224,1... | collective-permute-start | bytes 3145736 | tf_op jit(solution)/shard_map/ppermute | solution.py:17
  107.0 28.2 %copy-start.11 = (bf16[1,16,4096]{2,1,0:T(8,128)(2,1)S(1)}, bf16[1,16,4096]{2,1,0:T(8,128)(2,1)}, u32[]{:S(2)}) copy-start(bf16[1,16,4096]{2,1,0:T(8,128)(2,1)} %param.27) | copy-start | bytes 393220
  133.8 1.4 copy-start.1
  148.8 9.6 %collective-permute-start.2 = (bf16[1,512,256]{2,1,0:T(8,128)(2,1)S(1)}, bf16[1,512,256]{2,1,0:T(8,128)(2,1)S(1)}, u32[]{:S(2)}, u32[]{:S(2)}) collective-permute-start(bf16[1,512,256]{2,1,0:T(8,128)(2,1)S(1)} %bitcast.113), channel_id=1, source_target_pairs={{0,32},{32,0},{64,96},{96,64},{128,160},{160,128},{192,224},{224,1... | collective-permute-start | bytes 786440 | tf_op jit(solution)/shard_map/ppermute | solution.py:17
  159.2 27.4 %collective-permute-start.3 = (bf16[1024,256]{1,0:T(8,128)(2,1)}, bf16[1024,256]{1,0:T(8,128)(2,1)}, u32[]{:S(2)}, u32[]{:S(2)}) collective-permute-start(bf16[1024,256]{1,0:T(8,128)(2,1)} %bitcast.22), channel_id=1, source_target_pairs={{0,64},{32,96},{64,0},{96,32},{128,192},{160,224},{192,128},{224,1... | collective-permute-start | bytes 1572872 | tf_op jit(solution)/shard_map/ppermute | solution.py:17
  186.6 10.6 %copy-start.14 = (bf16[1,32,256]{2,1,0:T(8,128)(2,1)S(1)}, bf16[1,32,256]{2,1,0:T(8,128)(2,1)}, u32[]{:S(2)}) copy-start(bf16[1,32,256]{2,1,0:T(8,128)(2,1)} %param.19) | copy-start | bytes 49156
  214.5 14.9 %collective-permute-start.4 = (bf16[1,1024,256]{2,1,0:T(8,128)(2,1)S(1)}, bf16[1,1024,256]{2,1,0:T(8,128)(2,1)S(1)}, u32[]{:S(2)}, u32[]{:S(2)}) collective-permute-start(bf16[1,1024,256]{2,1,0:T(8,128)(2,1)S(1)} %bitcast.109), channel_id=1, source_target_pairs={{0,32},{32,0},{64,96},{96,64},{128,160},{160,128},{192,224},{224,1... | collective-permute-start | bytes 1572872 | tf_op jit(solution)/shard_map/ppermute | solution.py:17
  230.6 50.1 %collective-permute-start.5 = (bf16[2,1024,256]{2,1,0:T(8,128)(2,1)}, bf16[2,1024,256]{2,1,0:T(8,128)(2,1)}, u32[]{:S(2)}, u32[]{:S(2)}) collective-permute-start(bf16[2,1024,256]{2,1,0:T(8,128)(2,1)} %maximum_select_fusion.4), channel_id=1, source_target_pairs={{0,64},{32,96},{64,0},{96,32},{128,192},{160,224},{192,128},{224,1... | collective-permute-start | bytes 3145736 | tf_op jit(solution)/shard_map/ppermute | solution.py:17
  234.4 48.9 %copy-start.8 = (bf16[1,32,4096]{2,1,0:T(8,128)(2,1)S(1)}, bf16[1,32,4096]{2,1,0:T(8,128)(2,1)}, u32[]{:S(2)}) copy-start(bf16[1,32,4096]{2,1,0:T(8,128)(2,1)} %param.25) | copy-start | bytes 786436
  283.3 32.3 %copy-start.3 = (bf16[4,1024,256]{2,1,0:T(8,128)(2,1)}, bf16[4,1024,256]{2,1,0:T(8,128)(2,1)S(1)}, u32[]{:S(2)}) copy-start(bf16[4,1024,256]{2,1,0:T(8,128)(2,1)S(1)} %maximum_select_fusion.1) | copy-start | bytes 6291460
  283.7 83.8 %copy-start.12 = (bf16[256,32]{0,1:T(8,128)(2,1)}, bf16[256,32]{0,1:T(8,128)(2,1)S(1)}, u32[]{:S(2)}) copy-start(bf16[256,32]{0,1:T(8,128)(2,1)S(1)} %convolution_convert_fusion.2) | copy-start | bytes 49156
  300.4 14.9 %collective-permute-start.6 = (bf16[1,1024,256]{2,1,0:T(8,128)(2,1)S(1)}, bf16[1,1024,256]{2,1,0:T(8,128)(2,1)S(1)}, u32[]{:S(2)}, u32[]{:S(2)}) collective-permute-start(bf16[1,1024,256]{2,1,0:T(8,128)(2,1)S(1)} %bitcast.111), channel_id=1, source_target_pairs={{0,32},{32,0},{64,96},{96,64},{128,160},{160,128},{192,224},{224,1... | collective-permute-start | bytes 1572872 | tf_op jit(solution)/shard_map/ppermute | solution.py:17
  315.6 50.3 %collective-permute-start.7 = (bf16[2,1024,256]{2,1,0:T(8,128)(2,1)S(1)}, bf16[2,1024,256]{2,1,0:T(8,128)(2,1)S(1)}, u32[]{:S(2)}, u32[]{:S(2)}) collective-permute-start(bf16[2,1024,256]{2,1,0:T(8,128)(2,1)S(1)} %maximum_select_fusion.5), channel_id=1, source_target_pairs={{0,64},{32,96},{64,0},{96,32},{128,192},{160,224},{192,128},{224,1... | collective-permute-start | bytes 3145736 | tf_op jit(solution)/shard_map/ppermute | solution.py:17
  367.5 6.5 %copy-start.15 = (bf16[1,64,1024]{2,1,0:T(8,128)(2,1)S(1)}, bf16[1,64,1024]{2,1,0:T(8,128)(2,1)}, u32[]{:S(2)}) copy-start(bf16[1,64,1024]{2,1,0:T(8,128)(2,1)} %param.29) | copy-start | bytes 393220
  377.6 26.4 %copy-start.10 = (bf16[256,64]{0,1:T(8,128)(2,1)}, bf16[256,64]{0,1:T(8,128)(2,1)S(1)}, u32[]{:S(2)}) copy-start(bf16[256,64]{0,1:T(8,128)(2,1)S(1)} %fusion.8) | copy-start | bytes 98308
  378.8 22.1 %all-to-all-start.6 = ((bf16[32,1,64,256]{3,2,1,0:T(8,128)(2,1)}), bf16[32,1,64,256]{3,2,1,0:T(8,128)(2,1)}, u32[]{:S(2)}, u32[]{:S(2)}) async-start(bf16[32,1,64,256]{3,2,1,0:T(8,128)(2,1)} %stack.20), calls=%async_computation.6 | async-start | bytes 2097152 | tf_op jit(solution)/shard_map/all_to_all | solution.py:10
  400.9 3.2 copy-start.5
  400.9 26.6 %collective-permute-start.8 = (bf16[1,2048,256]{2,1,0:T(8,128)(2,1)}, bf16[1,2048,256]{2,1,0:T(8,128)(2,1)S(1)}, u32[]{:S(2)}, u32[]{:S(2)}) collective-permute-start(bf16[1,2048,256]{2,1,0:T(8,128)(2,1)} %bitcast.40), channel_id=1, source_target_pairs={{0,32},{32,0},{64,96},{96,64},{128,160},{160,128},{192,224},{224,1... | collective-permute-start | bytes 3145736 | tf_op jit(solution)/shard_map/ppermute | solution.py:17
  404.1 1.6 copy-start.2
  404.1 1.7 copy-start.6
  405.7 1.6 copy-start.4
  405.7 1.6 copy-start.9
